TPU v7x, 512 devices: a whole 4x8x8 slice. The times are simulated.
512 devices in a mesh: fsdp: 64 (over y, x, core), tensor: 8 (over z).
Axes of the slice: x: 4, y: 8, z: 8, core: 2. Of those that a mesh axis runs over, the one named last changes fastest.
Arguments:
- momentum: float32 [7168, 28672], P('fsdp', 'tensor'), may hold values from -6 to 6
- gradient: bfloat16 [7168, 28672], P('fsdp', 'tensor'), may hold values from -40 to 40
- basis_panel: float32 [256, 28672], P('fsdp', 'tensor'), may hold values from -0.625 to 0.625
Outputs:
- momentum_new: float32 [7168, 28672], P('fsdp', 'tensor')
- basis_new: float32 [256, 28672], P('fsdp', 'tensor')
- update: bfloat16 [7168, 28672], P('fsdp', 'tensor')
All inputs are finite; a program needn't handle non-finite values.
Results may differ from a plain program's by a relative error of at most 0.0012.
Values sent between devices are 32-bit elements; how exact they have to be, the bound alone decides.
No kernel may reach another device: no remote copies, remote signals or barrier semaphores. Data moves between devices by JAX's collectives and lax.ppermute only.
A program may use at most 64 MiB of HBM per device.

v0:
```python
import math
import jax
import jax.numpy as jnp
from jax import lax
from jax.sharding import PartitionSpec as P

ROWS = 7168
COLS = 28672
RANK = 256
norm_eps = 1e-06
carry_keep = 0.9


def shards(momentum, gradient, basis_panel):
    highest = lax.Precision.HIGHEST
    combined = momentum + gradient.astype(jnp.float32)
    panel_part = lax.dot_general(
        combined,
        lax.all_gather(basis_panel, "fsdp", axis=0, tiled=True),
        (((1,), (1,)), ((), ())),
        precision=highest,
        preferred_element_type=jnp.float32,
    )
    panel_full = lax.psum(panel_part, "tensor")
    panel_squares = jnp.sum(panel_full * panel_full, axis=0)
    update_scale = math.sqrt(ROWS * COLS / RANK)
    squares_all = lax.psum(panel_squares, "fsdp")
    left_panel = panel_full / jnp.sqrt(squares_all + norm_eps)[None, :]
    right_share = lax.psum_scatter(
        lax.dot_general(
            left_panel,
            combined,
            (((0,), (0,)), ((), ())),
            precision=highest,
            preferred_element_type=jnp.float32,
        ),
        "fsdp",
        scatter_dimension=0,
        tiled=True,
    )
    right_squares = lax.psum(jnp.sum(right_share * right_share, axis=1), "tensor")
    right_scale = jnp.sqrt(right_squares + norm_eps)[:, None]
    right_whole, scale_whole = (
        lax.all_gather(right_share, "fsdp", axis=0, tiled=True),
        lax.all_gather(right_scale, "fsdp", axis=0, tiled=True),
    )
    feedback_sum = jnp.dot(
        left_panel, right_whole, precision=highest, preferred_element_type=jnp.float32
    )
    update_sum = jnp.dot(
        left_panel, right_whole / scale_whole, precision=highest, preferred_element_type=jnp.float32
    )
    basis_share = right_share / right_scale
    momentum_new = combined - (1.0 - carry_keep) * feedback_sum
    update = (update_scale * update_sum).astype(jnp.bfloat16)
    return (momentum_new, basis_share, update)


def solution(mesh):
    return jax.shard_map(
        shards,
        mesh=mesh,
        in_specs=(P("fsdp", "tensor"), P("fsdp", "tensor"), P("fsdp", "tensor")),
        out_specs=(P("fsdp", "tensor"), P("fsdp", "tensor"), P("fsdp", "tensor")),
        check_vma=False,
    )
```

profile of v0, /device:TPU:1, one launch (start us, length us, event | category | flops | bytes accessed | tf_op | source)
XLA Modules:
  0.0 685.8 jit_solution(13984997624992476977)
XLA Ops:
  7.2 0.0 all-gather.6.cloned.1.call-start
  7.2 0.7 all-gather.6.cloned.1.call-update
  7.9 0.0 all-reduce.5.cloned.1.call-start
  8.0 92.9 %all-gather.6.cloned.1.call-done = f32[64,4,3584]{2,1,0:T(4,128)} async-done(((f32[1,4,3584]{2,1,0:T(4,128)}), f32[64,4,3584]{2,1,0:T(4,128)}) %all-gather.6.cloned.1.call-update) | async-done | bytes 3670032 | tf_op jit(solution)/shard_map/all_gather | solution.py:19
  100.9 5.3 reshape.14
  106.2 6.3 fusion.5
  112.6 0.0 all-reduce.7.cloned.1.call-start
  112.6 70.8 %all-reduce.5.cloned.1.call-done = f32[112,256]{1,0:T(8,128)} async-done(((f32[112,256]{1,0:T(8,128)}), f32[112,256]{1,0:T(8,128)}) %all-reduce.5.cloned.1.call-update) | async-done | bytes 114704 | tf_op jit(solution)/shard_map/psum | solution.py:24
  183.4 0.9 multiply_reduce_fusion
  184.3 128.8 %psum.22 = f32[256]{0:T(256)S(1)} all-reduce(f32[256]{0:T(256)S(1)} %multiply_reduce_fusion), channel_id=1, replica_groups=mesh['fsdp'=64,'tensor'=8] {'fsdp'}, use_global_device_ids=true, to_apply=%region_2.0 | all-reduce | flops 256 | bytes 2048 | tf_op jit(solution)/shard_map/psum | solution.py:27
  313.2 5.8 fusion.4
  319.0 0.0 all-gather.8.cloned.1.call-start
  319.1 0.6 copy-done.4
  319.7 0.6 fusion.7
  320.9 196.8 %all-reduce.7.cloned.1.call-done = f32[256,3584]{1,0:T(8,128)} async-done(((f32[256,3584]{1,0:T(8,128)}), f32[256,3584]{1,0:T(8,128)}) %all-reduce.7.cloned.1.call-update) | async-done | bytes 3670032
  517.8 1.0 multiply_reduce_fusion.1
  519.5 14.6 %psum.23 = f32[4]{0:T(128)S(1)} all-reduce(f32[4]{0:T(128)S(1)} %multiply_reduce_fusion.1), channel_id=1, replica_groups=mesh['fsdp'=64,'tensor'=8] {'tensor'}, use_global_device_ids=true, to_apply=%region_5.0 | all-reduce | flops 4 | bytes 32 | tf_op jit(solution)/shard_map/psum | solution.py:41
  534.1 0.1 fusion.6
  534.2 1.6 dynamic-slice_divide_fusion
  535.8 0.0 all-gather.8.cloned.1.call-update
  535.8 129.4 %all-reduce = f32[256]{0:T(256)S(1)} all-reduce(f32[256]{0:T(256)S(1)} %get-tuple-element.7), channel_id=2, replica_groups=mesh['fsdp'=64,'tensor'=8] {'fsdp'}, use_global_device_ids=true, to_apply=%add | all-reduce | flops 256 | bytes 2048
  665.3 5.3 reshape.16
  670.6 5.5 fusion
  676.1 3.2 fusion.1
  (14 shorter events, 0.1 us)
Async XLA Ops:
  7.2 93.7 %all-gather.6.cloned.1.call-start = ((), (), s32[]{:S(2)}) async-start(), calls=%async_computation.1 | async-start | bytes 3727360 | tf_op jit(solution)/shard_map/all_gather | solution.py:19
  7.9 98.3 %copy-start.1 = (f32[112,3584]{1,0:T(8,128)S(1)}, f32[112,3584]{1,0:T(8,128)}, u32[]{:S(2)}) copy-start(f32[112,3584]{1,0:T(8,128)} %param.3) | copy-start | bytes 4816900
  7.9 98.3 %copy-start.2 = (bf16[112,3584]{1,0:T(8,128)(2,1)S(1)}, bf16[112,3584]{1,0:T(8,128)(2,1)}, u32[]{:S(2)}) copy-start(bf16[112,3584]{1,0:T(8,128)(2,1)} %param.4) | copy-start | bytes 2408452
  7.9 175.5 %all-reduce.5.cloned.1.call-start = ((), (), s32[]{:S(2)}) async-start(), calls=%async_computation | async-start | bytes 229376 | tf_op jit(solution)/shard_map/psum | solution.py:24
  112.6 405.2 %all-reduce.7.cloned.1.call-start = ((), (), s32[]{:S(2)}) async-start(), calls=%async_computation.3 | async-start | bytes 7340032
  319.0 0.7 copy-start.4
  319.0 346.3 %all-gather.8.cloned.1.call-start = ((), (), s32[]{:S(2)}) async-start(), calls=%async_computation.2 | async-start | bytes 3727360 | tf_op jit(solution)/shard_map/all_gather | solution.py:44
  665.3 5.3 copy-start.3
  670.6 5.5 copy-start
Sparse Core Ops, SparseCore 0:
  11.3 89.5 all-gather.5
  112.7 70.6 all-reduce.4
  319.1 198.5 all-reduce.6
  536.0 85.3 all-gather.7
where the time goes:
time: 686 us
  waiting for transfers between devices  361 us (53%)
  blocking collectives  273 us (40%)
  matrix products  20.8 us (3%)
  between operations  15.1 us (2%)
  local copies, waits for them, and re-layouts  11.8 us (2%)
    unnamed x5, waiting for transfers between devices  198 us
    unnamed x1, blocking collectives  129 us
    psum x1, blocking collectives, shards(): squares_all = lax.psum(panel_squares, 'fsdp')  129 us
    all_gather x1, waiting for transfers between devices, shards(): lax.all_gather(basis_panel, 'fsdp', axis=0, tiled=True)  92.9 us
    psum x1, waiting for transfers between devices, shards(): panel_full = lax.psum(panel_part, 'tensor')  70.8 us
    psum x1, blocking collectives, shards(): lax.psum(jnp.sum(right_share * right_share, axis=1), 'tensor')  14.6 us
  transfers between devices with their start and end apart: 4, of which 3 were waited for; matrix products, arithmetic and copies ran while one was open for 0% of the time, Pallas kernels for 0%

commit v1 on v0

--- a/solution.py
+++ b/solution.py
@@ -21,7 +21,7 @@
         precision=highest,
         preferred_element_type=jnp.float32,
     )
-    panel_full = lax.psum(panel_part, "tensor")
+    panel_full = jnp.sum(lax.all_gather(panel_part, "tensor"), axis=0)
     panel_squares = jnp.sum(panel_full * panel_full, axis=0)
     update_scale = math.sqrt(ROWS * COLS / RANK)
     squares_all = lax.psum(panel_squares, "fsdp")

time: 686 us -> 636 us (0.927)
  waiting for transfers between devices: 361 us -> 290 us
  blocking collectives: 273 us -> 296 us
    psum x1 -> x0, waiting for transfers between devices: 70.8 us -> none  [shards(): panel_full = lax.psum(panel_part, 'tensor')]
    all_gather x0 -> x1, blocking collectives: none -> 23.2 us  [shards(): panel_full = jnp.sum(lax.all_gather(panel_part, 'tensor'), axis=0)]
    unnamed x5 -> x4, waiting for transfers between devices: 198 us -> 197 us
  transfers between devices with their start and end apart: 4 -> 3, of which waited for: 3 -> 2; matrix products, arithmetic and copies ran while one was open for 0% -> 0% of each run, Pallas kernels for 0% -> 0%
where the time goes in v1:
time: 636 us; the launch traced here: 635 us
  blocking collectives  296 us (47%)
  waiting for transfers between devices  290 us (46%)
  matrix products  19.3 us (3%)
  between operations  15.1 us (2%)
  local copies, waits for them, and re-layouts  11.8 us (2%)
    unnamed x4, waiting for transfers between devices  197 us
    unnamed x1, blocking collectives  129 us
    psum x1, blocking collectives, shards(): squares_all = lax.psum(panel_squares, 'fsdp')  129 us
    all_gather x1, waiting for transfers between devices, shards(): lax.all_gather(basis_panel, 'fsdp', axis=0, tiled=True)  92.9 us
    all_gather x1, blocking collectives, shards(): panel_full = jnp.sum(lax.all_gather(panel_part, 'tensor'), axis=0)  23.2 us
    psum x1, blocking collectives, shards(): lax.psum(jnp.sum(right_share * right_share, axis=1), 'tensor')  14.6 us
  transfers between devices with their start and end apart: 3, of which 2 were waited for; matrix products, arithmetic and copies ran while one was open for 0% of the time, Pallas kernels for 0%

profile of v1, /device:TPU:1, one launch (start us, length us, event | category | flops | bytes accessed | tf_op | source)
XLA Modules:
  0.0 635.2 jit_solution(6547540947940183674)
XLA Ops:
  7.2 0.0 all-gather.7.cloned.1.call-start
  7.2 0.7 all-gather.7.cloned.1.call-update
  7.9 0.0 all-reduce.4.cloned.1.call-start
  8.0 92.9 %all-gather.7.cloned.1.call-done = f32[64,4,3584]{2,1,0:T(4,128)} async-done(((f32[1,4,3584]{2,1,0:T(4,128)}), f32[64,4,3584]{2,1,0:T(4,128)}) %all-gather.7.cloned.1.call-update) | async-done | bytes 3670032 | tf_op jit(solution)/shard_map/all_gather | solution.py:19
  100.9 5.3 reshape.15
  106.2 5.7 fusion.5
  111.9 23.2 %all-gather = f32[896,256]{1,0:T(8,128)S(1)} all-gather(f32[112,256]{1,0:T(8,128)S(1)} %fusion.5), channel_id=2, replica_groups=mesh['fsdp'=64,'tensor'=8] {'tensor'}, dimensions={0}, use_global_device_ids=true | all-gather | bytes 1032192 | tf_op jit(solution)/shard_map/all_gather | solution.py:24
  135.1 0.1 reduce_sum.27
  135.2 128.9 %psum.14 = f32[256]{0:T(256)S(1)} all-reduce(f32[256]{0:T(256)S(1)} %multiply_reduce_fusion), channel_id=1, replica_groups=mesh['fsdp'=64,'tensor'=8] {'fsdp'}, use_global_device_ids=true, to_apply=%region_2.0 | all-reduce | flops 256 | bytes 2048 | tf_op jit(solution)/shard_map/psum | solution.py:27
  264.1 4.9 fusion.4
  269.0 0.0 all-reduce.4.cloned.1.call-update
  269.0 0.0 all-gather.9.cloned.1.call-start
  269.1 0.6 copy-done.3
  269.7 0.6 fusion.7
  270.9 196.2 %all-reduce.4.cloned.1.call-done = f32[256,3584]{1,0:T(8,128)} async-done(((f32[256,3584]{1,0:T(8,128)}), f32[256,3584]{1,0:T(8,128)}) %all-reduce.4.cloned.1.call-update) | async-done | bytes 3670032
  467.1 1.0 multiply_reduce_fusion.1
  468.8 14.6 %psum.15 = f32[4]{0:T(128)S(1)} all-reduce(f32[4]{0:T(128)S(1)} %multiply_reduce_fusion.1), channel_id=1, replica_groups=mesh['fsdp'=64,'tensor'=8] {'tensor'}, use_global_device_ids=true, to_apply=%region_5.0 | all-reduce | flops 4 | bytes 32 | tf_op jit(solution)/shard_map/psum | solution.py:41
  483.5 0.1 fusion.6
  483.6 1.6 dynamic-slice_divide_fusion
  485.2 0.0 all-gather.9.cloned.1.call-update
  485.2 129.4 %all-reduce = f32[256]{0:T(256)S(1)} all-reduce(f32[256]{0:T(256)S(1)} %get-tuple-element.7), channel_id=3, replica_groups=mesh['fsdp'=64,'tensor'=8] {'fsdp'}, use_global_device_ids=true, to_apply=%add | all-reduce | flops 256 | bytes 2048
  614.6 5.3 reshape.17
  619.9 5.5 fusion
  625.5 3.2 fusion.1
  (11 shorter events, 0.1 us)
Async XLA Ops:
  7.2 93.7 %all-gather.7.cloned.1.call-start = ((), (), s32[]{:S(2)}) async-start(), calls=%async_computation | async-start | bytes 3727360 | tf_op jit(solution)/shard_map/all_gather | solution.py:19
  7.9 98.3 %copy-start.1 = (f32[112,3584]{1,0:T(8,128)S(1)}, f32[112,3584]{1,0:T(8,128)}, u32[]{:S(2)}) copy-start(f32[112,3584]{1,0:T(8,128)} %param.3) | copy-start | bytes 4816900
  7.9 98.3 %copy-start.2 = (bf16[112,3584]{1,0:T(8,128)(2,1)S(1)}, bf16[112,3584]{1,0:T(8,128)(2,1)}, u32[]{:S(2)}) copy-start(bf16[112,3584]{1,0:T(8,128)(2,1)} %param.4) | copy-start | bytes 2408452
  7.9 459.2 %all-reduce.4.cloned.1.call-start = ((), (), s32[]{:S(2)}) async-start(), calls=%async_computation.2 | async-start | bytes 7340032
  269.0 0.7 copy-start.3
  269.0 345.6 %all-gather.9.cloned.1.call-start = ((), (), s32[]{:S(2)}) async-start(), calls=%async_computation.1 | async-start | bytes 3727360 | tf_op jit(solution)/shard_map/all_gather | solution.py:44
  619.9 5.5 copy-start
Sparse Core Ops, SparseCore 0:
  11.3 89.5 all-gather.6
  269.1 197.9 all-reduce.3
  485.3 85.3 all-gather.8
